TPU v7x, 32 devices: a whole 2x2x4 slice. The times are simulated.
32 devices in a mesh: plots: 8 (over y, x, core), band: 4 (over z).
Axes of the slice: x: 2, y: 2, z: 4, core: 2. Of those that a mesh axis runs over, the one named last changes fastest.
Arguments:
- patches: bfloat16 [32, 1024, 768], P('plots', 'band'), may hold values from -6 to 6
- norm1_gain: float32 [768], replicated, may hold values from 0.1 to 1.9
- w_query: bfloat16 [768, 768], replicated, may hold values from -0.4375 to 0.4375
- w_key: bfloat16 [768, 768], replicated, may hold values from -0.21875 to 0.21875
- w_value: bfloat16 [768, 768], replicated, may hold values from -0.21875 to 0.21875
- w_out: bfloat16 [768, 768], replicated, may hold values from -0.875 to 0.875
- norm2_gain: float32 [768], replicated, may hold values from 0.1 to 1.9
- w_gate: bfloat16 [768, 2048], replicated, may hold values from -0.21875 to 0.21875
- w_up: bfloat16 [768, 2048], replicated, may hold values from -0.21875 to 0.21875
- w_down: bfloat16 [2048, 768], replicated, may hold values from -0.25 to 0.25
- out_grad: bfloat16 [32, 1024, 768], P('plots', 'band'), may hold values from -6 to 6
- plot_rows: int32 [32], P('plots'), may hold values from 8 to 16, as said below
- plot_cols: int32 [32], P('plots'), may hold values from 32 to 64
- global_index: int32 [32, 128], P('plots'), may hold values from 0 to 1023, as said below
Outputs:
- mixed_out: bfloat16 [32, 1024, 768], P('plots', 'band')
- patch_grad: bfloat16 [32, 1024, 768], P('plots', 'band')
- norm1_grad: float32 [768], replicated
- query_grad: float32 [768, 768], replicated
- key_grad: float32 [768, 768], replicated
- value_grad: float32 [768, 768], replicated
- out_proj_grad: float32 [768, 768], replicated
- norm2_grad: float32 [768], replicated
- gate_grad: float32 [768, 2048], replicated
- up_grad: float32 [768, 2048], replicated
- down_grad: float32 [2048, 768], replicated
Inputs may be any that keep to these rules, and one draw needn't show every extreme that they name: `plot_rows`: in each aligned group of 4 plots one plot has 16 rows and 64 columns. `global_index`: A plot's 128 indices are distinct valid slots of that plot.
All inputs are finite; a program needn't handle non-finite values.
Results may differ from a plain program's by a relative error of at most 0.017.
The roundings to bfloat16 on the way count: a program that leaves them out, or rounds other values in their place, can miss the bound.
Values may be sent and summed in bfloat16 or wider, within the bound.
No kernel may reach another device: no remote copies, remote signals or barrier semaphores. Data moves between devices by JAX's collectives and lax.ppermute only.
A program may use at most 256 MiB of HBM per device.

v0:
```python
import jax
import jax.numpy as jnp
from jax import lax
from jax.sharding import PartitionSpec as P

H = 12
HD = 64
ROWS_DEV = 4
COLS = 64
WIN = 2


def extended(cells, sides, width):
    for axis, dim in sides:
        count = lax.axis_size(axis)
        ends = count - 1
        head = lax.slice_in_dim(cells, 0, width, axis=dim)
        tail = lax.slice_in_dim(cells, cells.shape[dim] - width, cells.shape[dim], axis=dim)
        cells = jnp.concatenate(
            [
                lax.ppermute(tail, axis, [(i, (i + 1) % count) for i in range(ends)]),
                cells,
                lax.ppermute(head, axis, [((i + 1) % count, i) for i in range(ends)]),
            ],
            axis=dim,
        )
    return cells


def rms_norm(values, gain):
    inverse = lax.rsqrt(jnp.mean(values * values, axis=-1, keepdims=True) + 1e-06)
    return values * inverse * gain


def linear(left, weight):
    return jnp.einsum("ptd,de->pte", left, weight, preferred_element_type=jnp.float32)


def linear_back(grad, weight):
    return jnp.einsum("pte,de->ptd", grad, weight, preferred_element_type=jnp.float32)


def outer(left, right):
    return jnp.einsum("ptd,pte->de", left, right, preferred_element_type=jnp.float32)


def masked_scores(query, keys, allowed):
    raw = jnp.einsum("qhd,khd->hqk", query, keys, preferred_element_type=jnp.float32) * HD ** (-0.5)
    return jnp.where(allowed[None], raw, -1e30)


def attend(operands):
    query, keys, values, allowed = operands
    scores = masked_scores(query, keys, allowed)
    highest = jnp.max(scores, axis=-1, keepdims=True)
    expont = jnp.exp(scores - highest)
    total = jnp.sum(expont, axis=-1, keepdims=True)
    probs = (expont / total).astype(jnp.bfloat16)
    attended = jnp.einsum("hqk,khd->qhd", probs, values, preferred_element_type=jnp.float32)
    return (attended.reshape(query.shape[0], -1).astype(jnp.bfloat16), highest + jnp.log(total))


def attend_back(operands):
    query, keys, values, allowed, log_total, grad_heads = operands
    probs = jnp.exp(masked_scores(query, keys, allowed) - log_total)
    grad_probs = jnp.einsum("qhd,khd->hqk", grad_heads, values, preferred_element_type=jnp.float32)
    weighted = jnp.sum(probs * grad_probs, axis=-1, keepdims=True)
    grad_scores = (probs * (grad_probs - weighted)).astype(jnp.bfloat16)
    grad_query = jnp.einsum(
        "hqk,khd->qhd", grad_scores, keys, preferred_element_type=jnp.float32
    ) * HD ** (-0.5)
    grad_keys = jnp.einsum(
        "hqk,qhd->khd", grad_scores, query, preferred_element_type=jnp.float32
    ) * HD ** (-0.5)
    grad_values = jnp.einsum(
        "hqk,qhd->khd", probs.astype(jnp.bfloat16), grad_heads, preferred_element_type=jnp.float32
    )
    key_count = keys.shape[0]
    joined = jnp.concatenate(
        [grad_keys.reshape(key_count, -1), grad_values.reshape(key_count, -1)], 1
    )
    return (grad_query.reshape(query.shape[0], -1), joined)


def per_device(
    patches,
    norm1_gain,
    w_query,
    w_key,
    w_value,
    w_out,
    norm2_gain,
    w_gate,
    w_up,
    w_down,
    out_grad,
    plot_rows,
    plot_cols,
    global_index,
):
    plots_here, band_slots, width = patches.shape
    globals_here = global_index.shape[1]
    band_index = lax.axis_index("band")
    band_count = lax.axis_size("band")
    window_slots = (ROWS_DEV + 2 * WIN) * COLS
    key_count = window_slots + globals_here
    inputs = patches.astype(jnp.float32)
    hidden = rms_norm(inputs, norm1_gain).astype(jnp.bfloat16)
    query = linear(hidden, w_query).astype(jnp.bfloat16)
    keys = linear(hidden, w_key).astype(jnp.bfloat16)
    values = linear(hidden, w_value).astype(jnp.bfloat16)
    joined = jnp.concatenate([keys, values], 2)
    widened = extended(joined.reshape(plots_here, ROWS_DEV, COLS, 2 * width), (("band", 1),), WIN)
    widened = widened.reshape(plots_here, window_slots, 2 * width)
    local_slot = global_index - band_index * band_slots
    picker = local_slot[:, :, None] == jnp.arange(band_slots, dtype=jnp.int32)[None, None, :]
    chosen = jnp.einsum(
        "pgt,pte->pge", picker.astype(jnp.bfloat16), joined, preferred_element_type=jnp.float32
    ).astype(jnp.bfloat16)
    collected = lax.all_gather(chosen[None], "band", axis=0, tiled=True)
    global_rows = jnp.sum(collected.astype(jnp.float32), 0).astype(jnp.bfloat16)
    all_keys = jnp.concatenate([widened, global_rows], 1)
    key_heads = all_keys[..., :width].reshape(plots_here, key_count, H, HD)
    value_heads = all_keys[..., width:].reshape(plots_here, key_count, H, HD)
    position = jnp.arange(window_slots, dtype=jnp.int32)
    key_row = band_index * ROWS_DEV - WIN + position // COLS
    key_col = position % COLS
    inside = (
        (key_row[None, :] >= 0)
        & (key_row[None, :] < plot_rows[:, None])
        & (key_col[None, :] < plot_cols[:, None])
    )
    query_row = band_index * ROWS_DEV + jnp.arange(band_slots, dtype=jnp.int32) // COLS
    near = jnp.abs(key_row[None, :] - query_row[:, None]) <= WIN
    allowed = jnp.concatenate(
        [
            near[None] & inside[:, None, :],
            jnp.ones((plots_here, band_slots, globals_here), dtype=bool),
        ],
        2,
    )
    query_heads = query.reshape(plots_here, band_slots, H, HD)
    attended, log_total = lax.map(attend, (query_heads, key_heads, value_heads, allowed))
    resid = inputs + linear(attended, w_out)
    hidden2 = rms_norm(resid, norm2_gain).astype(jnp.bfloat16)
    gate = linear(hidden2, w_gate)
    up_proj = linear(hidden2, w_up)
    activated, gelu_back = jax.vjp(lambda value_in: jax.nn.gelu(value_in, approximate=True), gate)
    inner = (activated * up_proj).astype(jnp.bfloat16)
    mixed_out = (resid + linear(inner, w_down)).astype(jnp.bfloat16)
    grad_down = outer(inner, out_grad)
    grad_inner = linear_back(out_grad, w_down)
    grad_gate = gelu_back(grad_inner * up_proj)[0].astype(jnp.bfloat16)
    grad_up = (grad_inner * activated).astype(jnp.bfloat16)
    grad_w_gate = outer(hidden2, grad_gate)
    grad_w_up = outer(hidden2, grad_up)
    grad_hidden2 = linear_back(grad_gate, w_gate) + linear_back(grad_up, w_up)
    norm2_back = jax.vjp(rms_norm, resid, norm2_gain)[1]
    grad_resid, grad_norm2 = norm2_back(grad_hidden2)
    grad_resid = grad_resid + out_grad.astype(jnp.float32)
    resid_low = grad_resid.astype(jnp.bfloat16)
    grad_w_out = outer(attended, resid_low)
    grad_attended = (
        linear_back(resid_low, w_out).astype(jnp.bfloat16).reshape(plots_here, band_slots, H, HD)
    )
    grad_query, grad_joined = lax.map(
        attend_back, (query_heads, key_heads, value_heads, allowed, log_total, grad_attended)
    )
    window_grad = grad_joined[:, :window_slots].reshape(
        plots_here, ROWS_DEV + 2 * WIN, COLS, 2 * width
    )
    global_grad = grad_joined[:, window_slots:]
    edges = jnp.concatenate([window_grad[:, :WIN], window_grad[:, ROWS_DEV + WIN :]], 1)
    returned = extended(edges.astype(jnp.bfloat16), (("band", 1),), WIN).astype(edges.dtype)
    own_grad = window_grad[:, WIN : WIN + ROWS_DEV]
    own_grad = own_grad.at[:, :WIN].add(returned[:, :WIN])
    own_grad = own_grad.at[:, ROWS_DEV - WIN :].add(returned[:, 3 * WIN :])
    owner = global_index // band_slots
    holders = owner[None] == jnp.arange(band_count, dtype=jnp.int32)[:, None, None]
    terms = jnp.where(holders[..., None], global_grad[None], 0.0)
    summed = lax.psum_scatter(
        terms.astype(jnp.bfloat16), "band", scatter_dimension=0, tiled=True
    ).astype(jnp.float32)[0]
    placed = jnp.einsum(
        "pgt,pge->pte", picker.astype(jnp.float32), summed, precision=lax.Precision.HIGHEST
    )
    grad_kv = own_grad.reshape(plots_here, band_slots, 2 * width) + placed
    grad_key_low = grad_kv[..., :width].astype(jnp.bfloat16)
    grad_value_low = grad_kv[..., width:].astype(jnp.bfloat16)
    grad_query_low = grad_query.astype(jnp.bfloat16)
    grad_w_query = outer(hidden, grad_query_low)
    grad_w_key = outer(hidden, grad_key_low)
    grad_w_value = outer(hidden, grad_value_low)
    grad_hidden = (
        linear_back(grad_query_low, w_query)
        + linear_back(grad_key_low, w_key)
        + linear_back(grad_value_low, w_value)
    )
    norm1_back = jax.vjp(rms_norm, inputs, norm1_gain)[1]
    grad_inputs, grad_norm1 = norm1_back(grad_hidden)
    patch_grad = (grad_inputs + grad_resid).astype(jnp.bfloat16)
    pieces = [
        grad_norm1,
        grad_w_query,
        grad_w_key,
        grad_w_value,
        grad_w_out,
        grad_norm2,
        grad_w_gate,
        grad_w_up,
        grad_down,
    ]
    flattened = jnp.concatenate([piece.reshape(-1) for piece in pieces])
    length = flattened.shape[0]
    device_count = lax.axis_size("plots") * band_count
    stride = 128 * device_count
    padded_length = (length + stride - 1) // stride * stride
    dealt = jnp.pad(flattened, (0, padded_length - length)).reshape(-1, device_count, 128)
    matrix = jnp.transpose(dealt, (1, 0, 2)).reshape(-1, 128)
    reduced = lax.psum_scatter(matrix, ("plots", "band"), scatter_dimension=0, tiled=True)
    whole_sum = lax.all_gather(
        reduced.astype(jnp.bfloat16), ("plots", "band"), axis=0, tiled=True
    ).astype(reduced.dtype)
    summed_flat = jnp.transpose(whole_sum.reshape(device_count, -1, 128), (1, 0, 2)).reshape(-1)
    results = []
    offset = 0
    for piece in pieces:
        count = piece.size
        results.append(summed_flat[offset : offset + count].reshape(piece.shape))
        offset = offset + count
    return (
        mixed_out,
        patch_grad,
        results[0],
        results[1],
        results[2],
        results[3],
        results[4],
        results[5],
        results[6],
        results[7],
        results[8],
    )


def solution(mesh):
    in_specs = (
        P("plots", "band", None),
        P(),
        P(),
        P(),
        P(),
        P(),
        P(),
        P(),
        P(),
        P(),
        P("plots", "band", None),
        P("plots"),
        P("plots"),
        P("plots", None),
    )
    out_specs = (
        P("plots", "band", None),
        P("plots", "band", None),
        P(),
        P(),
        P(),
        P(),
        P(),
        P(),
        P(),
        P(),
        P(),
    )
    return jax.shard_map(
        per_device, mesh=mesh, in_specs=in_specs, out_specs=out_specs, check_vma=False
    )
```

profile of v0, /device:TPU:0, one launch (start us, length us, event | category | flops | bytes accessed | tf_op | source)
XLA Modules:
  0.0 1654.4 jit_solution(4589535512968953921)
XLA Ops:
  9.8 4.5 convolution_convert_fusion.3
  17.5 3.7 convolution_convert_fusion
  27.3 6.7 collective-permute-start
  34.1 4.6 convolution_convert_fusion.2
  43.9 9.2 fusion.67
  53.1 73.4 %collective-permute-done.1 = bf16[4,2,64,1536]{3,2,1,0:T(8,128)(2,1)} collective-permute-done((bf16[4,2,64,1536]{3,2,1,0:T(8,128)(2,1)}, bf16[4,2,64,1536]{3,2,1,0:T(8,128)(2,1)}, u32[]{:S(2)}, u32[]{:S(2)}) %collective-permute-start.1) | collective-permute-done | bytes 1572896 | tf_op jit(solution)/shard_map/ppermute | solution.py:23
  126.5 5.1 pad_maximum_fusion
  131.6 8.6 copy.77
  140.2 28.2 %all-gather.5.cloned.1.call-done = bf16[16,128,1536]{2,1,0:T(8,128)(2,1)} async-done(((bf16[4,128,1536]{2,1,0:T(8,128)(2,1)}), bf16[16,128,1536]{2,1,0:T(8,128)(2,1)}) %all-gather.5.cloned.1.call-update) | async-done | bytes 6291472 | tf_op jit(solution)/shard_map/all_gather | solution.py:120
  168.4 5.4 reduce_sum.87
  176.3 5.7 pad_maximum_fusion.1
  182.0 40.5 %while.26 = (s32[]{:T(128)}, bf16[4,256,768]{1,2,0:T(8,128)(2,1)}, f32[4,12,256,1]{2,1,3,0:T(8,128)S(1)}, bf16[4,640,12,64]{1,3,2,0:T(8,128)(2,1)}, pred[4,256,6...) while((s32[]{:T(128)}, bf16[4,256,768]{1,2,0:T(8,128)(2,1)}, ...), condition=%wide.region_5.6_spmd, body=%wide.region_2.5_spmd.sunk | while | flops 527102976 | bytes 28062828 | solution.py:143
  187.8 3.5 fusion.166
  197.9 3.5 fusion.166
  208.0 3.5 fusion.166
  218.2 3.5 fusion.166
  222.5 3.9 multiply_reduce_fusion.3
  229.5 5.9 fusion.73
  235.3 13.4 fusion.53
  248.7 7.7 fusion.71
  256.4 4.6 multiply_reduce_fusion.1
  267.5 79.6 %while.27 = (s32[]{:T(128)}, bf16[4,256,768]{1,2,0:T(8,128)(2,1)}, f32[4,640,1536]{1,2,0:T(8,128)}, bf16[4,640,12,64]{1,3,2,0:T(8,128)(2,1)}, pred[4,256,640]{2,...) while((s32[]{:T(128)}, bf16[4,256,768]{1,2,0:T(8,128)(2,1)}, ...), condition=%wide.region_10.11_spmd, body=%wide.region_8.10_spmd.sunk | while | flops 1289647104 | bytes 83687576 | solution.py:166
  271.4 4.5 multiply_reduce_fusion.5
  291.3 4.5 multiply_reduce_fusion.5
  311.1 4.5 multiply_reduce_fusion.5
  330.9 4.5 multiply_reduce_fusion.5
  350.0 3.5 select_convert_fusion
  353.6 15.8 copy.83
  369.4 10.3 slice.159
  379.7 6.1 slice.160
  385.8 8.2 convert.14
  397.7 7.1 collective-permute-start.2
  411.1 5.2 convolution_bitcast_fusion.3
  419.5 5.8 convolution_bitcast_fusion.2
  425.3 4.2 copy.104
  433.0 4.1 copy.105
  437.1 5.5 convolution_bitcast_fusion
  442.7 7.1 reshape.407
  449.8 4.8 fusion.92
  454.6 44.4 %collective-permute-done.3 = bf16[4,2,64,1536]{3,2,1,0:T(8,128)(2,1)} collective-permute-done((bf16[4,2,64,1536]{3,2,1,0:T(8,128)(2,1)S(1)}, bf16[4,2,64,1536]{3,2,1,0:T(8,128)(2,1)}, u32[]{:S(2)}, u32[]{:S(2)}) %collective-permute-start.3) | collective-permute-done | bytes 1572896 | tf_op jit(solution)/shard_map/ppermute | solution.py:23
  499.0 4.6 fusion.66
  503.6 4.6 fusion.65
  508.1 4.3 fusion.54
  528.1 6.8 fusion.59
  536.2 21.3 %dynamic-update-slice.7 = f32[7079424]{0:T(1024)} dynamic-update-slice(f32[7079424]{0:T(1024)} %constant_dynamic-update-slice_fusion.3, f32[589824]{0:T(1024)} %reshape.401, s32[]{} %constant.219) | dynamic-update-slice | bytes 4718596
  557.5 21.3 %dynamic-update-slice.8 = f32[7079424]{0:T(1024)} dynamic-update-slice(f32[7079424]{0:T(1024)} %dynamic-update-slice.7, f32[589824]{0:T(1024)} %reshape.402, s32[]{} %constant.220) | dynamic-update-slice | bytes 4718596
  578.7 21.3 %dynamic-update-slice.9 = f32[7079424]{0:T(1024)} dynamic-update-slice(f32[7079424]{0:T(1024)} %dynamic-update-slice.8, f32[589824]{0:T(1024)} %reshape.403, s32[]{} %constant.221) | dynamic-update-slice | bytes 4718596
  600.0 21.3 %dynamic-update-slice.10 = f32[7079424]{0:T(1024)} dynamic-update-slice(f32[7079424]{0:T(1024)} %dynamic-update-slice.9, f32[589824]{0:T(1024)} %reshape.404, s32[]{} %constant.222) | dynamic-update-slice | bytes 4718596
  622.7 54.2 %dynamic-update-slice.12 = f32[7079424]{0:T(1024)} dynamic-update-slice(f32[7079424]{0:T(1024)} %constant_dynamic-update-slice_fusion.2, f32[1572864]{0:T(1024)} %bitcast.220, s32[]{} %constant.224) | dynamic-update-slice | bytes 12582916
  676.9 54.2 %dynamic-update-slice.13 = f32[7079424]{0:T(1024)} dynamic-update-slice(f32[7079424]{0:T(1024)} %dynamic-update-slice.12, f32[1572864]{0:T(1024)} %bitcast.221, s32[]{} %constant.225) | dynamic-update-slice | bytes 12582916
  731.1 54.0 %dynamic-update-slice.14 = f32[7079424]{0:T(1024)} dynamic-update-slice(f32[7079424]{0:T(1024)} %dynamic-update-slice.13, f32[1572864]{0:T(1024)} %reshape.407, s32[]{} %constant.226) | dynamic-update-slice | bytes 12582916 | tf_op jit(solution)/shard_map/concatenate | solution.py:213
  785.1 11.3 pad.9
  796.4 18.6 %copy.92 = f32[32,1729,128]{2,1,0:T(8,128)} copy(f32[32,1729,128]{2,0,1:T(8,128)S(1)} %bitcast.208) | data formatting | bytes 56655872 | tf_op jit(solution)/shard_map/transpose | solution.py:219
  815.0 25.3 %reshape.409 = f32[55328,128]{1,0:T(8,128)} reshape(f32[32,1729,128]{2,1,0:T(8,128)} %copy.92) | data formatting | bytes 56655872 | tf_op jit(solution)/shard_map/reshape | solution.py:219
  840.3 612.5 %fusion = f32[1744,128]{1,0:T(8,128)S(1)} fusion(f32[55328,128]{1,0:T(8,128)} %reshape.409), kind=kCustom, calls=%all-reduce-scatter | all-reduce-scatter fusion | flops 7143425 | bytes 29220864
  1459.0 8.7 add_convert_fusion
  1469.8 93.2 %all-gather.7.cloned.1.call-done = bf16[32,1729,128]{2,1,0:T(8,128)(2,1)} async-done(((bf16[1,1729,128]{2,1,0:T(8,128)(2,1)}), bf16[32,1729,128]{2,1,0:T(8,128)(2,1)}) %all-gather.7.cloned.1.call-update) | async-done | bytes 14163984 | tf_op jit(solution)/shard_map/all_gather | solution.py:221
  1563.0 20.9 %copy_convert_fusion = f32[32,1729,128]{2,0,1:T(8,128)S(1)} fusion(bf16[32,1729,128]{2,1,0:T(8,128)(2,1)} %all-gather.7.cloned.1.call-done), kind=kLoop, calls=%fused_computation.60 | loop fusion | flops 7081984 | bytes 42491904 | tf_op jit(solution)/shard_map/reshape | solution.py:224
  1583.9 9.3 copy-done.2
  1593.9 6.9 fusion.127
  1600.8 13.7 fusion.125
  1626.2 7.1 reshape.417
  1633.2 7.1 reshape.418
  1640.3 7.4 reshape.419
  (209 shorter events, 174.9 us)
Async XLA Ops:
  7.2 228.2 %copy-start = (bf16[768,2048]{1,0:T(8,128)(2,1)S(1)}, bf16[768,2048]{1,0:T(8,128)(2,1)}, u32[]{:S(2)}) copy-start(bf16[768,2048]{1,0:T(8,128)(2,1)} %param.29) | copy-start | bytes 9437188
  7.2 161.2 %all-gather.5.cloned.1.call-start = ((), (), s32[]{:S(2)}) async-start(), calls=%async_computation.2 | async-start | bytes 7864320 | tf_op jit(solution)/shard_map/all_gather | solution.py:120
  9.2 0.6 copy-start.24
  9.8 24.3 %copy-start.22 = (f32[4,256]{1,0:T(4,128)}, f32[4,256]{1,0:T(4,128)S(1)}, u32[]{:S(2)}) copy-start(f32[4,256]{1,0:T(4,128)S(1)} %fusion.110) | copy-start | bytes 12292
  9.8 4.5 copy-start.5
  9.8 4.5 copy-start.26
  9.8 4.5 copy-start.39
  14.3 2.6 copy-start.33
  17.0 0.6 copy-start.29
  21.2 486.9 %reduce-scatter.4.cloned.1.call-start = ((), (), s32[]{:S(2)}) async-start(), calls=%async_computation.1 | async-start | bytes 7864320 | tf_op jit(solution)/shard_map/reduce_scatter | solution.py:181
  23.4 2.7 copy-start.3
  26.0 100.4 %collective-permute-start.1 = (bf16[4,2,64,1536]{3,2,1,0:T(8,128)(2,1)}, bf16[4,2,64,1536]{3,2,1,0:T(8,128)(2,1)}, u32[]{:S(2)}, u32[]{:S(2)}) collective-permute-start(bf16[4,2,64,1536]{3,2,1,0:T(8,128)(2,1)} %get-tuple-element.198), channel_id=1, source_target_pairs={{1,0},{2,1},{3,2},{5,4},{6,5},{7,6},{9,8},{10,9},{11,10},{13,12},{... | collective-permute-start | bytes 4718600 | tf_op jit(solution)/shard_map/ppermute | solution.py:23
  27.3 99.1 %collective-permute-start = (bf16[4,2,64,1536]{3,2,1,0:T(8,128)(2,1)}, bf16[4,2,64,1536]{3,2,1,0:T(8,128)(2,1)}, u32[]{:S(2)}, u32[]{:S(2)}) collective-permute-start(bf16[4,2,64,1536]{3,2,1,0:T(8,128)(2,1)} %get-tuple-element.197), channel_id=1, source_target_pairs={{0,1},{1,2},{2,3},{4,5},{5,6},{6,7},{8,9},{9,10},{10,11},{12,13},{... | collective-permute-start | bytes 4718600 | tf_op jit(solution)/shard_map/ppermute | solution.py:21
  34.1 4.6 copy-start.34
  34.1 4.6 copy-start.35
  43.9 82.6 %copy-start.4 = (bf16[4,256,1536]{2,1,0:T(8,128)(2,1)S(1)}, bf16[4,256,1536]{2,1,0:T(8,128)(2,1)}, u32[]{:S(2)}) copy-start(bf16[4,256,1536]{2,1,0:T(8,128)(2,1)} %copy-done.3) | copy-start | bytes 9437188
  222.5 3.9 copy-start.28
  226.4 34.7 %copy-start.13 = (f32[4,256,768]{2,1,0:T(8,128)}, f32[4,256,768]{2,1,0:T(8,128)S(1)}, u32[]{:S(2)}) copy-start(f32[4,256,768]{2,1,0:T(8,128)S(1)} %get-tuple-element.202) | copy-start | bytes 9437188
  226.4 3.0 copy-start.36
  229.5 5.9 copy-start.8
  248.7 7.7 copy-start.16
  248.7 7.7 copy-start.18
  256.4 4.7 copy-start.19
  261.1 1.3 copy-start.38
  262.4 2.6 copy-start.10
  267.7 3.6 copy-start.14
  287.6 3.6 copy-start.14
  307.5 3.6 copy-start.14
  327.3 3.6 copy-start.14
  347.2 2.8 copy-start.31
  353.6 1209.4 %all-gather.7.cloned.1.call-start = ((), (), s32[]{:S(2)}) async-start(), calls=%async_computation.3 | async-start | bytes 14665728 | tf_op jit(solution)/shard_map/all_gather | solution.py:221
  394.0 10.7 copy-start.6
  394.0 10.8 copy-start.23
  394.0 10.8 copy-start.27
  394.0 10.8 copy-start.37
  396.4 102.6 %collective-permute-start.3 = (bf16[4,2,64,1536]{3,2,1,0:T(8,128)(2,1)S(1)}, bf16[4,2,64,1536]{3,2,1,0:T(8,128)(2,1)}, u32[]{:S(2)}, u32[]{:S(2)}) collective-permute-start(bf16[4,2,64,1536]{3,2,1,0:T(8,128)(2,1)S(1)} %get-tuple-element.196), channel_id=1, source_target_pairs={{1,0},{2,1},{3,2},{5,4},{6,5},{7,6},{9,8},{10,9},{11,10},{13,12},{... | collective-permute-start | bytes 4718600 | tf_op jit(solution)/shard_map/ppermute | solution.py:23
  397.7 101.3 %collective-permute-start.2 = (bf16[4,2,64,1536]{3,2,1,0:T(8,128)(2,1)S(1)}, bf16[4,2,64,1536]{3,2,1,0:T(8,128)(2,1)}, u32[]{:S(2)}, u32[]{:S(2)}) collective-permute-start(bf16[4,2,64,1536]{3,2,1,0:T(8,128)(2,1)S(1)} %get-tuple-element.195), channel_id=1, source_target_pairs={{0,1},{1,2},{2,3},{4,5},{5,6},{6,7},{8,9},{9,10},{10,11},{12,13},{... | collective-permute-start | bytes 4718600 | tf_op jit(solution)/shard_map/ppermute | solution.py:21
  425.3 4.2 copy-start.9
  425.3 4.2 copy-start.17
  433.0 4.1 copy-start.20
  433.0 4.1 copy-start.41
  503.6 4.6 copy-start.30
  508.1 4.3 copy-start.40
  512.4 6.1 copy-start.15
  512.5 3.1 copy-start.7
  524.8 3.3 copy-start.21
  600.0 21.3 %copy-start.32 = (f32[768]{0:T(1024)S(1)}, f32[768]{0:T(1024)}, u32[]{:S(2)}) copy-start(f32[768]{0:T(1024)} %get-tuple-element.141) | copy-start | bytes 9220
  1452.8 3.7 collective-permute-start.4
  1459.0 8.8 copy-start.25
  1459.0 8.8 copy-start.11
  1459.0 8.8 copy-start.12
  1583.9 9.3 copy-start.2
  1640.3 7.4 copy-start.1
Sparse Core Ops, SparseCore 0:
  21.4 147.0 all-gather.4
  353.7 145.0 reduce-scatter.3
  1459.1 103.8 all-gather.6
where the time goes:
time: 1680 us; the launch traced here: 1650 us
  blocking collectives  612 us (36%)
  local copies, waits for them, and re-layouts  476 us (28%)
  waiting for transfers between devices  242 us (14%)
  matrix products  200 us (12%)
  other arithmetic  91.8 us (5%)
  starting transfers between devices  17.8 us (1%)
    unnamed x1, blocking collectives  612 us
    unnamed x95, local copies, waits for them, and re-layouts  221 us
    ppermute x2, waiting for transfers between devices, extended(): lax.ppermute(head, axis, [((i + 1) % count, i) for i in range(ends)])  118 us
    all_gather x1, waiting for transfers between devices, per_device(): lax.all_gather(reduced.astype(jnp.bfloat16), ('plots', 'band'), axis=0, t...  93.2 us
    concatenate x1, local copies, waits for them, and re-layouts, per_device(): flattened = jnp.concatenate([piece.reshape(-1) for piece in pieces])  54 us
    dot_general x7, matrix products, linear(): jnp.einsum('ptd,de->pte', left, weight, preferred_element_type=jnp.float32)  43.6 us
    dot_general x7, matrix products, linear_back(): jnp.einsum('pte,de->ptd', grad, weight, preferred_element_type=jnp.float32)  38.9 us
  transfers between devices with their start and end apart: 8, of which 5 were waited for; matrix products, arithmetic and copies ran while one was open for 9% of the time, Pallas kernels for 0%

commit v1 on v0

v1 whole, which is shorter than its diff:
```python
import functools

import jax
import jax.numpy as jnp
from jax import lax
from jax.experimental import pallas as pl
from jax.experimental.pallas import tpu as pltpu
from jax.sharding import PartitionSpec as P

H = 12
HD = 64
COLS = 64
WIN = 2
TILE_ROWS = 4
PAIR = 2 * HD
BF = jnp.bfloat16
F32 = jnp.float32
LOG2E = 1.4426950408889634
SCALE2 = LOG2E * HD ** (-0.5)


def dot_nt(a, b):
    return lax.dot_general(a, b, (((1,), (1,)), ((), ())), preferred_element_type=F32)


def dot_nn(a, b):
    return lax.dot_general(a, b, (((1,), (0,)), ((), ())), preferred_element_type=F32)


def dot_tn(a, b):
    return lax.dot_general(a, b, (((0,), (0,)), ((), ())), preferred_element_type=F32)


def tiles_of(rows):
    out = []
    for first in range(0, rows, TILE_ROWS):
        low = max(first - WIN, 0)
        high = min(first + TILE_ROWS + WIN, rows)
        out.append((first * COLS, low * COLS, high * COLS))
    return out


def fill_bias(bias_ref, limits_ref, tiles):
    rows_here = limits_ref[0]
    cols_here = limits_ref[1]
    for number, (query_lo, key_lo, key_hi) in enumerate(tiles):
        count = key_hi - key_lo
        shape = (count, TILE_ROWS * COLS)
        key = lax.broadcasted_iota(jnp.int32, shape, 0) + key_lo
        query = lax.broadcasted_iota(jnp.int32, shape, 1) + query_lo
        key_row = key // COLS
        apart = key_row - query // COLS
        seen = (apart <= WIN) & (apart >= -WIN) & (key_row < rows_here) & (key % COLS < cols_here)
        bias_ref[number, :count, :] = jnp.where(seen, 0.0, -1e30).astype(F32)


def picker_rows(index_ref, slots):
    chosen = index_ref[:, 0:1]
    lanes = lax.broadcasted_iota(jnp.int32, (chosen.shape[0], slots), 1)
    return (lanes == chosen).astype(F32).astype(BF)


def attend_kernel(
    limits_ref, index_ref, q_ref, k_ref, v_ref, out_ref, lse_ref, bias_ref, pick_ref, value_t
):
    slots = q_ref.shape[0]
    tiles = tiles_of(slots // COLS)
    span = TILE_ROWS * COLS

    @pl.when(pl.program_id(0) == 0)
    def _():
        fill_bias(bias_ref, limits_ref, tiles)
        pick_ref[...] = picker_rows(index_ref, slots)

    global_keys = dot_nn(pick_ref[...], k_ref[...]).astype(BF)
    global_values = dot_nn(pick_ref[...], v_ref[...])
    global_values_t = jnp.transpose(global_values).astype(BF)
    value_t[...] = jnp.transpose(v_ref[...].astype(F32)).astype(BF)
    lane = lax.broadcasted_iota(jnp.int32, (span, PAIR), 1)
    for number, (query_lo, key_lo, key_hi) in enumerate(tiles):
        count = key_hi - key_lo
        query = q_ref[query_lo : query_lo + span, :]
        heads = []
        for half in range(2):
            masked = jnp.where((lane < HD) == (half == 0), query, jnp.zeros_like(query))
            window = dot_nt(k_ref[key_lo:key_hi, :], masked) * SCALE2 + bias_ref[number, :count, :]
            wide = dot_nt(global_keys, masked) * SCALE2
            highest = jnp.maximum(
                jnp.max(window, axis=0, keepdims=True), jnp.max(wide, axis=0, keepdims=True)
            )
            window = jnp.exp2(window - highest)
            wide = jnp.exp2(wide - highest)
            total = jnp.sum(window, axis=0, keepdims=True) + jnp.sum(wide, axis=0, keepdims=True)
            inverse = 1.0 / total
            window = (window * inverse).astype(BF)
            wide = (wide * inverse).astype(BF)
            rows = slice(half * HD, half * HD + HD)
            heads.append(
                dot_nn(value_t[rows, key_lo:key_hi], window) + dot_nn(global_values_t[rows, :], wide)
            )
            lse_ref[0, half : half + 1, query_lo : query_lo + span] = highest + jnp.log2(total)
        joined = jnp.concatenate(heads, axis=0)
        out_ref[query_lo : query_lo + span, :] = jnp.transpose(joined).astype(BF)


def attend_back_kernel(
    limits_ref,
    index_ref,
    index_t_ref,
    q_ref,
    k_ref,
    v_ref,
    g_ref,
    lse_ref,
    dq_ref,
    dk_ref,
    dv_ref,
    bias_ref,
    pick_ref,
    pick_t_ref,
    key_t,
    dk_acc,
    dv_acc,
):
    slots = q_ref.shape[0]
    tiles = tiles_of(slots // COLS)
    span = TILE_ROWS * COLS
    globals_here = index_ref.shape[0]

    @pl.when(pl.program_id(0) == 0)
    def _():
        fill_bias(bias_ref, limits_ref, tiles)
        pick_ref[...] = picker_rows(index_ref, slots)
        down = lax.broadcasted_iota(jnp.int32, (slots, globals_here), 0)
        pick_t_ref[...] = (down == index_t_ref[0:1, :]).astype(F32).astype(BF)

    global_keys_f = dot_nn(pick_ref[...], k_ref[...])
    global_keys = global_keys_f.astype(BF)
    global_keys_t = jnp.transpose(global_keys_f).astype(BF)
    global_values = dot_nn(pick_ref[...], v_ref[...]).astype(BF)
    key_t[...] = jnp.transpose(k_ref[...].astype(F32)).astype(BF)
    dk_acc[...] = jnp.zeros_like(dk_acc)
    dv_acc[...] = jnp.zeros_like(dv_acc)
    dk_global = jnp.zeros((globals_here, PAIR), F32)
    dv_global = jnp.zeros((globals_here, PAIR), F32)
    lane = lax.broadcasted_iota(jnp.int32, (span, PAIR), 1)
    for number, (query_lo, key_lo, key_hi) in enumerate(tiles):
        count = key_hi - key_lo
        query = q_ref[query_lo : query_lo + span, :]
        grad = g_ref[query_lo : query_lo + span, :]
        keys = k_ref[key_lo:key_hi, :]
        values = v_ref[key_lo:key_hi, :]
        heads = []
        for half in range(2):
            mine = (lane < HD) == (half == 0)
            query_m = jnp.where(mine, query, jnp.zeros_like(query))
            grad_m = jnp.where(mine, grad, jnp.zeros_like(grad))
            lse = lse_ref[0, half : half + 1, query_lo : query_lo + span]
            window = jnp.exp2(dot_nt(keys, query_m) * SCALE2 + (bias_ref[number, :count, :] - lse))
            wide = jnp.exp2(dot_nt(global_keys, query_m) * SCALE2 - lse)
            window_g = dot_nt(values, grad_m)
            wide_g = dot_nt(global_values, grad_m)
            weighted = jnp.sum(window * window_g, axis=0, keepdims=True) + jnp.sum(
                wide * wide_g, axis=0, keepdims=True
            )
            window_s = (window * (window_g - weighted)).astype(BF)
            wide_s = (wide * (wide_g - weighted)).astype(BF)
            dv_acc[key_lo:key_hi, :] += dot_nn(window.astype(BF), grad_m)
            dk_acc[key_lo:key_hi, :] += dot_nn(window_s, query_m)
            dv_global += dot_nn(wide.astype(BF), grad_m)
            dk_global += dot_nn(wide_s, query_m)
            rows = slice(half * HD, half * HD + HD)
            heads.append(
                dot_nn(key_t[rows, key_lo:key_hi], window_s) + dot_nn(global_keys_t[rows, :], wide_s)
            )
        joined = jnp.concatenate(heads, axis=0) * HD ** (-0.5)
        dq_ref[query_lo : query_lo + span, :] = jnp.transpose(joined).astype(BF)

    def spread(part):
        high = part.astype(BF)
        rest = part - high.astype(F32)
        middle = rest.astype(BF)
        low = (rest - middle.astype(F32)).astype(BF)
        picks = pick_t_ref[...]
        return dot_nn(picks, high) + dot_nn(picks, middle) + dot_nn(picks, low)

    dk_ref[...] = ((dk_acc[...] + spread(dk_global)) * HD ** (-0.5)).astype(BF)
    dv_ref[...] = (dv_acc[...] + spread(dv_global)).astype(BF)


def attention_parts(slots, width, globals_here):
    pairs = width // PAIR
    tall = (TILE_ROWS + 2 * WIN) * COLS
    tiles = slots // (TILE_ROWS * COLS)
    limits = pl.BlockSpec(memory_space=pltpu.SMEM)
    index = pl.BlockSpec((globals_here, 128), lambda p: (0, 0))
    block = pl.BlockSpec((slots, PAIR), lambda p: (0, p))
    lse = pl.BlockSpec((1, 8, slots), lambda p: (p, 0, 0))
    bias = pltpu.VMEM((tiles, tall, TILE_ROWS * COLS), F32)
    pick = pltpu.VMEM((globals_here, slots), BF)
    return pairs, limits, index, block, lse, bias, pick


def attention(query, keys, values, limits, index):
    slots, width = query.shape
    globals_here = index.shape[0]
    pairs, lim, idx, block, lse, bias, pick = attention_parts(slots, width, globals_here)
    return pl.pallas_call(
        attend_kernel,
        grid=(pairs,),
        in_specs=[lim, idx, block, block, block],
        out_specs=[block, lse],
        out_shape=[
            jax.ShapeDtypeStruct((slots, width), BF),
            jax.ShapeDtypeStruct((pairs, 8, slots), F32),
        ],
        scratch_shapes=[bias, pick, pltpu.VMEM((PAIR, slots), BF)],
        compiler_params=pltpu.CompilerParams(vmem_limit_bytes=40 * 2**20),
        name="attend",
    )(limits, index, query, keys, values)


def attention_back(query, keys, values, grad, lse_in, limits, index, index_t):
    slots, width = query.shape
    globals_here = index.shape[0]
    pairs, lim, idx, block, lse, bias, pick = attention_parts(slots, width, globals_here)
    idx_t = pl.BlockSpec((8, globals_here), lambda p: (0, 0))
    low = jax.ShapeDtypeStruct((slots, width), BF)
    return pl.pallas_call(
        attend_back_kernel,
        grid=(pairs,),
        in_specs=[lim, idx, idx_t, block, block, block, block, lse],
        out_specs=[block, block, block],
        out_shape=[low, low, low],
        scratch_shapes=[
            bias,
            pick,
            pltpu.VMEM((slots, globals_here), BF),
            pltpu.VMEM((PAIR, slots), BF),
            pltpu.VMEM((slots, PAIR), F32),
            pltpu.VMEM((slots, PAIR), F32),
        ],
        compiler_params=pltpu.CompilerParams(vmem_limit_bytes=40 * 2**20),
        name="attend_back",
    )(limits, index, index_t, query, keys, values, grad, lse_in)


def flip(axis, bit):
    count = lax.axis_size(axis)
    return [(i, i ^ bit) for i in range(count)]


def take(array, number, axis=0):
    return lax.dynamic_index_in_dim(array, number, axis, keepdims=False)


def add_low(left, right):
    return (left.astype(F32) + right.astype(F32)).astype(BF)


def swap_to_plots(blocks):
    count = lax.axis_size("band")
    here = lax.axis_index("band")
    got = [take(blocks, here)]
    for bit in range(1, count):
        got.append(lax.ppermute(take(blocks, here ^ bit), "band", flip("band", bit)))
    stacked = jnp.stack(got)
    return jnp.concatenate([take(stacked, here ^ band) for band in range(count)])


def swap_to_bands(whole):
    count = lax.axis_size("band")
    here = lax.axis_index("band")
    blocks = whole.reshape(count, whole.shape[0] // count, whole.shape[1])
    got = [take(blocks, here)]
    for bit in range(1, count):
        got.append(lax.ppermute(take(blocks, here ^ bit), "band", flip("band", bit)))
    stacked = jnp.stack(got)
    return jnp.stack([take(stacked, here ^ plot) for plot in range(count)])


def stages(reverse):
    plots = lax.axis_size("plots")
    band = lax.axis_size("band")
    bits = [("plots", 1 << n) for n in range(plots.bit_length() - 1)]
    tail = [("band", 1 << n) for n in range(band.bit_length() - 1)]
    first, rest = bits[:1], bits[1:]
    return first + (rest[::-1] if reverse else rest) + tail


def scatter_sum(matrix, order):
    for axis, bit in order:
        mine = (lax.axis_index(axis) // bit) % 2
        halves = matrix.reshape(2, matrix.shape[0] // 2, matrix.shape[1])
        arrived = lax.ppermute(take(halves, 1 - mine), axis, flip(axis, bit))
        matrix = add_low(take(halves, mine), arrived)
    return matrix


def gather_all(matrix, order):
    for axis, bit in order[::-1]:
        mine = (lax.axis_index(axis) // bit) % 2
        other = lax.ppermute(matrix, axis, flip(axis, bit))
        matrix = jnp.where(
            mine == 0,
            jnp.concatenate([matrix, other]),
            jnp.concatenate([other, matrix]),
        )
    return matrix


def rms_norm(values, gain):
    inverse = lax.rsqrt(jnp.mean(values * values, axis=-1, keepdims=True) + 1e-06)
    return values * inverse * gain


def per_device(
    patches,
    norm1_gain,
    w_query,
    w_key,
    w_value,
    w_out,
    norm2_gain,
    w_gate,
    w_up,
    w_down,
    out_grad,
    plot_rows,
    plot_cols,
    global_index,
):
    width = patches.shape[2]
    here = lax.axis_index("band")
    x_low = swap_to_plots(patches)
    dy = swap_to_plots(out_grad)
    limits = jnp.stack([take(plot_rows, here), take(plot_cols, here)])
    chosen = take(global_index, here)
    index = jnp.broadcast_to(chosen[:, None], (chosen.shape[0], 128))
    index_t = jnp.broadcast_to(chosen[None, :], (8, chosen.shape[0]))

    inputs = x_low.astype(F32)
    hidden = rms_norm(inputs, norm1_gain).astype(BF)
    query = dot_nn(hidden, w_query).astype(BF)
    keys = dot_nn(hidden, w_key).astype(BF)
    values = dot_nn(hidden, w_value).astype(BF)
    attended, lse = attention(query, keys, values, limits, index)
    resid = inputs + dot_nn(attended, w_out)
    hidden2 = rms_norm(resid, norm2_gain).astype(BF)
    gate = dot_nn(hidden2, w_gate)
    up_proj = dot_nn(hidden2, w_up)
    activated, gelu_back = jax.vjp(lambda value_in: jax.nn.gelu(value_in, approximate=True), gate)
    inner = (activated * up_proj).astype(BF)
    mixed_out = (resid + dot_nn(inner, w_down)).astype(BF)
    mixed_out = swap_to_bands(mixed_out)
    grad_down_t = dot_tn(dy, inner)
    grad_inner = dot_nt(dy, w_down)
    grad_gate = gelu_back(grad_inner * up_proj)[0].astype(BF)
    grad_up = (grad_inner * activated).astype(BF)
    grad_w_gate = dot_tn(hidden2, grad_gate)
    grad_w_up = dot_tn(hidden2, grad_up)
    grad_hidden2 = dot_nt(grad_gate, w_gate) + dot_nt(grad_up, w_up)
    norm2_back = jax.vjp(rms_norm, resid, norm2_gain)[1]
    grad_resid, grad_norm2 = norm2_back(grad_hidden2)
    grad_resid = grad_resid + dy.astype(F32)
    resid_low = grad_resid.astype(BF)
    grad_w_out = dot_tn(attended, resid_low)
    grad_attended = dot_nt(resid_low, w_out).astype(BF)
    first = jnp.concatenate([grad_w_gate, grad_w_up, grad_down_t, grad_w_out], 1).astype(BF)
    order = stages(False)
    first = scatter_sum(first, order)

    grad_query, grad_keys, grad_values = attention_back(
        query, keys, values, grad_attended, lse, limits, index, index_t
    )
    grad_w_query = dot_tn(hidden, grad_query)
    grad_w_key = dot_tn(hidden, grad_keys)
    grad_w_value = dot_tn(hidden, grad_values)
    second = jnp.concatenate([grad_w_query, grad_w_key, grad_w_value], 1).astype(BF)
    other = stages(True)
    second = scatter_sum(second, other)
    grad_hidden = (
        dot_nt(grad_query, w_query) + dot_nt(grad_keys, w_key) + dot_nt(grad_values, w_value)
    )
    norm1_back = jax.vjp(rms_norm, inputs, norm1_gain)[1]
    grad_inputs, grad_norm1 = norm1_back(grad_hidden)
    patch_grad = (grad_inputs + grad_resid).astype(BF)
    patch_grad = swap_to_bands(patch_grad)
    gains = lax.psum(jnp.stack([grad_norm1, grad_norm2]), ("plots", "band"))

    first = gather_all(first, order).astype(F32)
    second = gather_all(second, other).astype(F32)
    ff = w_gate.shape[1]
    return (
        mixed_out,
        patch_grad,
        gains[0],
        second[:, :width],
        second[:, width : 2 * width],
        second[:, 2 * width :],
        first[:, 3 * ff :],
        gains[1],
        first[:, :ff],
        first[:, ff : 2 * ff],
        jnp.transpose(first[:, 2 * ff : 3 * ff]),
    )


def solution(mesh):
    rows = P("plots", "band", None)
    in_specs = (rows,) + (P(),) * 9 + (rows, P("plots"), P("plots"), P("plots", None))
    out_specs = (rows, rows) + (P(),) * 9
    return jax.shard_map(
        per_device, mesh=mesh, in_specs=in_specs, out_specs=out_specs, check_vma=False
    )
```

time: 1680 us -> 612 us (0.36); the launches traced: 1650 us -> 608 us
  blocking collectives: 612 us -> 44.9 us
  local copies, waits for them, and re-layouts: 476 us -> 59.7 us
  matrix products: 200 us -> 82.9 us
  Pallas kernels: 0 us -> 58 us
  other arithmetic: 91.8 us -> 59.9 us
  starting transfers between devices: 17.8 us -> 42.3 us
    unnamed x1 -> x0, blocking collectives: 612 us -> none
    unnamed x95 -> x131, local copies, waits for them, and re-layouts: 221 us -> 25.7 us
    ppermute x4 -> x32, waiting for transfers between devices: 118 us -> 258 us  [the longest x10 97.5 us: scatter_sum(): arrived = lax.ppermute(take(halves, 1 - mine), axis, flip(axis, bit))]
    all_gather x2 -> x0, waiting for transfers between devices: 121 us -> none  [the longest x1 93.2 us: per_device(): lax.all_gather(reduced.astype(jnp.bfloat16), ('plots', 'band'), axis=0, t...]
    dot_general x51 -> x21, matrix products: 200 us -> 82.9 us  [the longest x7 37.8 us: dot_nt(): lax.dot_general(a, b, (((1,), (1,)), ((), ())), preferred_element_type=F32)]
    reshape x14 -> x2, local copies, waits for them, and re-layouts: 87.1 us -> 0.01 us  [rms_norm(): return values * inverse * gain]
    pallas_call x0 -> x2, Pallas kernels: none -> 58 us  [the longest x1 34 us: attention_back(): pl.pallas_call(attend_back_kernel, grid=(pairs,), in_specs=[lim, idx, idx...]
    concatenate x2 -> x0, local copies, waits for them, and re-layouts: 54.9 us -> none  [the longest x1 54 us: per_device(): flattened = jnp.concatenate([piece.reshape(-1) for piece in pieces])]
  transfers between devices with their start and end apart: 8 -> 32, of which waited for: 5 -> 18; matrix products, arithmetic and copies ran while one was open for 9% -> 12% of each run, Pallas kernels for 0% -> 6%
where the time goes in v1:
time: 612 us; the launch traced here: 608 us
  waiting for transfers between devices  258 us (42%)
  matrix products  82.9 us (14%)
  other arithmetic  59.9 us (10%)
  local copies, waits for them, and re-layouts  59.7 us (10%)
  Pallas kernels  58 us (9%)
  blocking collectives  44.9 us (7%)
  starting transfers between devices  42.3 us (7%)
    ppermute x10, waiting for transfers between devices, scatter_sum(): arrived = lax.ppermute(take(halves, 1 - mine), axis, flip(axis, bit))  97.5 us
    ppermute x10, waiting for transfers between devices, gather_all(): other = lax.ppermute(matrix, axis, flip(axis, bit))  88.8 us
    psum x1, blocking collectives, per_device(): gains = lax.psum(jnp.stack([grad_norm1, grad_norm2]), ('plots', 'band'))  44.9 us
    ppermute x6, waiting for transfers between devices, swap_to_plots(): lax.ppermute(take(blocks, here ^ bit), 'band', flip('band', bit))  41.8 us
    dot_general x7, matrix products, dot_nt(): lax.dot_general(a, b, (((1,), (1,)), ((), ())), preferred_element_type=F32)  37.8 us
    pallas_call x1, Pallas kernels, attention_back(): pl.pallas_call(attend_back_kernel, grid=(pairs,), in_specs=[lim, idx, idx...  34 us
    ppermute x6, waiting for transfers between devices, swap_to_bands(): lax.ppermute(take(blocks, here ^ bit), 'band', flip('band', bit))  29.6 us
    unnamed x131, local copies, waits for them, and re-layouts  25.7 us
  transfers between devices with their start and end apart: 32, of which 18 were waited for; matrix products, arithmetic and copies ran while one was open for 12% of the time, Pallas kernels for 6%

profile of v1, /device:TPU:0, one launch (start us, length us, event | category | flops | bytes accessed | tf_op | source)
XLA Modules:
  0.0 607.6 jit_solution(2738165632977814855)
XLA Ops:
  0.7 2.7 constant_dynamic-slice_fusion.12
  3.4 3.0 collective-permute-start
  6.4 2.5 collective-permute-start.2
  10.0 1.8 collective-permute-start.6
  11.8 2.5 collective-permute-start.8
  17.5 9.5 %collective-permute-start.7 = (bf16[256,768]{1,0:T(8,128)(2,1)}, bf16[256,768]{1,0:T(8,128)(2,1)S(1)}, u32[]{:S(2)}, u32[]{:S(2)}) collective-permute-start(bf16[256,768]{1,0:T(8,128)(2,1)} %get-tuple-element.73), channel_id=1, source_target_pairs={{0,2},{1,3},{2,0},{3,1},{4,6},{5,7},{6,4},{7,5},{8,10},{9,11},{10,... | collective-permute-start | bytes 1179656 | tf_op jit(solution)/shard_map/ppermute | solution.py:266
  27.7 33.7 %collective-permute-done.1 = bf16[256,768]{1,0:T(8,128)(2,1)} collective-permute-done((bf16[256,768]{1,0:T(8,128)(2,1)}, bf16[256,768]{1,0:T(8,128)(2,1)}, u32[]{:S(2)}, u32[]{:S(2)}) %collective-permute-start.1) | collective-permute-done | bytes 393248 | tf_op jit(solution)/shard_map/ppermute | solution.py:266
  69.6 7.4 %collective-permute-done.7 = bf16[256,768]{1,0:T(8,128)(2,1)S(1)} collective-permute-done((bf16[256,768]{1,0:T(8,128)(2,1)}, bf16[256,768]{1,0:T(8,128)(2,1)S(1)}, u32[]{:S(2)}, u32[]{:S(2)}) %collective-permute-start.7) | collective-permute-done | bytes 393248 | tf_op jit(solution)/shard_map/ppermute | solution.py:266
  79.6 24.0 %attend.1 = (bf16[1024,768]{1,0:T(8,128)(2,1)S(1)}, f32[6,8,1024]{2,1,0:T(8,128)S(1)}) custom-call(s32[2]{0:T(128)S(1)} %pad_add_fusion.limits_ref, s32[128,128]{1,0:T(8,128)S(1)} %broadcast_in_dim.11.index_ref, bf16[1024,768]{1,0:T(8,128)(2,1)S(1)} %convolution_convert_fusion.6.q_ref, bf16[1024,768]{1,0:T(8,128)(2,1)S(1)} %convolution_convert_fusion.5.k_ref, ...), custom_call_target="tpu_custom_call" | custom-call | tf_op jit(solution)/shard_map/attend/pallas_call | solution.py:208
  105.6 2.7 copy-done.50
  108.3 5.7 fusion.42
  114.0 5.7 fusion.41
  119.7 16.1 %multiply_convert_fusion = (bf16[1024,2048]{1,0:T(8,128)(2,1)}, bf16[1024,2048]{1,0:T(8,128)(2,1)}, bf16[1024,2048]{1,0:T(8,128)(2,1)}) fusion(f32[1024,2048]{1,0:T(8,128)} %fusion.41, f32[1024,2048]{1,0:T(8,128)} %fusion.42, bf16[2048,768]{1,0:T(8,128)(2,1)S(1)} %copy-done, bf16[256,768]{1,0:T(8,128)(2,1)} %get-tuple-element.67, ...), kind=kOutput, calls=%fused_computation.14 | convolution fusion | flops 3282042880 | bytes 34078720 | tf_op jit(solution)/shard_map/dot_general | solution.py:23
  135.8 6.3 %convolution_convert_fusion.2 = bf16[768,2048]{1,0:T(8,128)(2,1)S(1)} fusion(bf16[1024,768]{1,0:T(8,128)(2,1)} %copy-done.40, bf16[1024,2048]{1,0:T(8,128)(2,1)} %get-tuple-element.53), kind=kOutput, calls=%fused_computation.38 | convolution fusion | flops 3222798336 | bytes 8912896 | tf_op jit(solution)/shard_map/dot_general | solution.py:31
  142.2 5.1 fusion.43
  147.3 3.8 convolution_convert_fusion
  151.1 4.9 convolution_convert_fusion.1
  156.0 4.0 multiply_reduce_fusion
  160.0 3.7 fusion.16
  167.6 2.9 dynamic-slice_bitcast_fusion
  170.5 2.6 copy-done.14
  173.2 9.1 %collective-permute-done.22 = bf16[384,6912]{1,0:T(8,128)(2,1)} collective-permute-done((bf16[384,6912]{1,0:T(8,128)(2,1)}, bf16[384,6912]{1,0:T(8,128)(2,1)}, u32[]{:S(2)}, u32[]{:S(2)}) %collective-permute-start.22) | collective-permute-done | bytes 5308448 | tf_op jit(solution)/shard_map/ppermute | solution.py:295
  182.3 5.3 fusion.1
  187.6 2.4 copy-done.15
  189.9 1.6 dynamic-slice_bitcast_fusion.1
  193.1 3.8 convolution_convert_fusion.3.g_ref
  196.9 34.0 %attend_back.1 = (bf16[1024,768]{1,0:T(8,128)(2,1)S(1)}, bf16[1024,768]{1,0:T(8,128)(2,1)S(1)}, bf16[1024,768]{1,0:T(8,128)(2,1)S(1)}) custom-call(s32[2]{0:T(128)S(1)} %pad_add_fusion.limits_ref, s32[128,128]{1,0:T(8,128)S(1)} %broadcast_in_dim.11.index_ref, s32[8,128]{1,0:T(8,128)S(1)} %broadcast_in_dim.12.index_t_ref, bf16[1024,768]{1,0:T(8,128)(2,1)S(1)} %copy-done.6, ...), custom_call_target="tpu_custom_call" | custom-call | tf_op jit(solution)/shard_map/attend_back/pallas_call | solution.py:229
  231.0 20.5 %collective-permute-done.23 = bf16[192,6912]{1,0:T(8,128)(2,1)} collective-permute-done((bf16[192,6912]{1,0:T(8,128)(2,1)}, bf16[192,6912]{1,0:T(8,128)(2,1)}, u32[]{:S(2)}, u32[]{:S(2)}) %collective-permute-start.23) | collective-permute-done | bytes 2654240 | tf_op jit(solution)/shard_map/ppermute | solution.py:295
  251.5 2.4 fusion.9
  254.0 1.6 collective-permute-start.24
  255.6 1.6 convolution_convert_fusion.10
  257.2 1.6 convolution_convert_fusion.9
  258.8 1.6 convolution_convert_fusion.8
  260.5 23.9 %collective-permute-done.24 = bf16[96,6912]{1,0:T(8,128)(2,1)S(1)} collective-permute-done((bf16[96,6912]{1,0:T(8,128)(2,1)S(1)}, bf16[96,6912]{1,0:T(8,128)(2,1)S(1)}, u32[]{:S(2)}, u32[]{:S(2)}) %collective-permute-start.24) | collective-permute-done | bytes 1327136 | tf_op jit(solution)/shard_map/ppermute | solution.py:295
  285.3 14.7 %collective-permute-done.25 = bf16[48,6912]{1,0:T(8,128)(2,1)S(1)} collective-permute-done((bf16[48,6912]{1,0:T(8,128)(2,1)S(1)}, bf16[48,6912]{1,0:T(8,128)(2,1)S(1)}, u32[]{:S(2)}, u32[]{:S(2)}) %collective-permute-start.25) | collective-permute-done | bytes 663584 | tf_op jit(solution)/shard_map/ppermute | solution.py:295
  302.3 13.2 %collective-permute-done.26 = bf16[24,6912]{1,0:T(8,128)(2,1)S(1)} collective-permute-done((bf16[24,6912]{1,0:T(8,128)(2,1)S(1)}, bf16[24,6912]{1,0:T(8,128)(2,1)S(1)}, u32[]{:S(2)}, u32[]{:S(2)}) %collective-permute-start.26) | collective-permute-done | bytes 331808 | tf_op jit(solution)/shard_map/ppermute | solution.py:295
  318.8 15.5 %collective-permute-done.27 = bf16[24,6912]{1,0:T(8,128)(2,1)} collective-permute-done((bf16[24,6912]{1,0:T(8,128)(2,1)}, bf16[24,6912]{1,0:T(8,128)(2,1)}, u32[]{:S(2)}, u32[]{:S(2)}) %collective-permute-start.27) | collective-permute-done | bytes 331808 | tf_op jit(solution)/shard_map/ppermute | solution.py:303
  335.8 3.3 collective-permute-done.13
  339.1 1.6 fusion.22
  340.8 1.6 collective-permute-start.14
  342.4 10.2 %collective-permute-done.28 = bf16[48,6912]{1,0:T(8,128)(2,1)S(1)} collective-permute-done((bf16[48,6912]{1,0:T(8,128)(2,1)S(1)}, bf16[48,6912]{1,0:T(8,128)(2,1)S(1)}, u32[]{:S(2)}, u32[]{:S(2)}) %collective-permute-start.28) | collective-permute-done | bytes 663584 | tf_op jit(solution)/shard_map/ppermute | solution.py:303
  357.3 6.3 %collective-permute-done.15 = bf16[48,2304]{1,0:T(8,128)(2,1)} collective-permute-done((bf16[48,2304]{1,0:T(8,128)(2,1)}, bf16[48,2304]{1,0:T(8,128)(2,1)}, u32[]{:S(2)}, u32[]{:S(2)}) %collective-permute-start.15) | collective-permute-done | bytes 221216 | tf_op jit(solution)/shard_map/ppermute | solution.py:295
  364.7 19.8 %collective-permute-done.29 = bf16[96,6912]{1,0:T(8,128)(2,1)} collective-permute-done((bf16[96,6912]{1,0:T(8,128)(2,1)}, bf16[96,6912]{1,0:T(8,128)(2,1)}, u32[]{:S(2)}, u32[]{:S(2)}) %collective-permute-start.29) | collective-permute-done | bytes 1327136 | tf_op jit(solution)/shard_map/ppermute | solution.py:303
  384.4 4.2 maximum_select_fusion.3
  390.7 6.5 %collective-permute-done.16 = bf16[24,2304]{1,0:T(8,128)(2,1)S(1)} collective-permute-done((bf16[24,2304]{1,0:T(8,128)(2,1)S(1)}, bf16[24,2304]{1,0:T(8,128)(2,1)S(1)}, u32[]{:S(2)}, u32[]{:S(2)}) %collective-permute-start.16) | collective-permute-done | bytes 110624 | tf_op jit(solution)/shard_map/ppermute | solution.py:295
  397.8 6.1 %collective-permute-done.17 = bf16[24,2304]{1,0:T(8,128)(2,1)} collective-permute-done((bf16[24,2304]{1,0:T(8,128)(2,1)}, bf16[24,2304]{1,0:T(8,128)(2,1)}, u32[]{:S(2)}, u32[]{:S(2)}) %collective-permute-start.17) | collective-permute-done | bytes 110624 | tf_op jit(solution)/shard_map/ppermute | solution.py:303
  405.1 6.6 %add_convert_fusion = bf16[1024,768]{1,0:T(8,128)(2,1)S(1)} fusion(f32[1024,768]{1,0:T(8,128)} %copy-done.19, bf16[1024,2048]{1,0:T(8,128)(2,1)} %get-tuple-element.54, bf16[2048,768]{1,0:T(8,128)(2,1)S(1)} %copy-done), kind=kOutput, calls=%fused_computation.49 | convolution fusion | flops 3222798336 | bytes 12058624 | tf_op jit(solution)/shard_map/dot_general | solution.py:27
  412.5 37.1 %collective-permute-done.30 = bf16[192,6912]{1,0:T(8,128)(2,1)} collective-permute-done((bf16[192,6912]{1,0:T(8,128)(2,1)}, bf16[192,6912]{1,0:T(8,128)(2,1)}, u32[]{:S(2)}, u32[]{:S(2)}) %collective-permute-start.30) | collective-permute-done | bytes 2654240 | tf_op jit(solution)/shard_map/ppermute | solution.py:303
  449.6 7.5 %maximum_select_fusion.1 = bf16[384,6912]{1,0:T(8,128)(2,1)} fusion(bf16[192,6912]{1,0:T(8,128)(2,1)} %collective-permute-done.30, bf16[192,6912]{1,0:T(8,128)(2,1)} %maximum_select_fusion.3, pred[]{:T(512)S(6)} %eq.43), kind=kLoop, calls=%fused_computation.23 | loop fusion | flops 23887872 | bytes 10616833 | tf_op jit(solution)/shard_map/jit(_where)/select_n | solution.py:304
  466.2 2.3 collective-permute-start.3
  468.5 6.0 fusion.15
  475.1 44.9 %psum.7 = f32[2,768]{1,0:T(2,128)S(1)} all-reduce(f32[2,768]{1,0:T(2,128)} %pad_maximum_fusion.10), channel_id=1, replica_groups=mesh['plots'=8,'band'=4] {'plots','band'}, use_global_device_ids=true, to_apply=%region_6.7 | all-reduce | flops 1536 | bytes 12288 | tf_op jit(solution)/shard_map/psum | solution.py:389
  520.0 2.5 maximum_select_fusion.4
  523.4 3.3 fusion.18
  526.8 2.4 collective-permute-start.11
  529.2 2.1 collective-permute-start.9
  533.5 7.3 %collective-permute-done.11 = bf16[256,768]{1,0:T(8,128)(2,1)S(1)} collective-permute-done((bf16[256,768]{1,0:T(8,128)(2,1)S(1)}, bf16[256,768]{1,0:T(8,128)(2,1)S(1)}, u32[]{:S(2)}, u32[]{:S(2)}) %collective-permute-start.11) | collective-permute-done | bytes 393248 | tf_op jit(solution)/shard_map/ppermute | solution.py:277
  540.8 22.3 %collective-permute-done.10 = bf16[256,768]{1,0:T(8,128)(2,1)S(1)} collective-permute-done((bf16[256,768]{1,0:T(8,128)(2,1)S(1)}, bf16[256,768]{1,0:T(8,128)(2,1)S(1)}, u32[]{:S(2)}, u32[]{:S(2)}) %collective-permute-start.10) | collective-permute-done | bytes 393248 | tf_op jit(solution)/shard_map/ppermute | solution.py:277
  563.3 1.9 pad_maximum_fusion.5
  566.0 3.1 fusion.40
  569.1 9.0 %fusion = f32[768,6912]{1,0:T(8,128)S(1)} fusion(bf16[384,6912]{1,0:T(8,128)(2,1)} %collective-permute-done.31, bf16[384,6912]{1,0:T(8,128)(2,1)} %maximum_select_fusion.1, pred[]{:T(512)S(6)} %eq.41), kind=kLoop, calls=%fused_computation.4 | loop fusion | flops 53084160 | bytes 31850496 | tf_op jit(solution)/shard_map/convert_element_type | solution.py:391
  578.1 7.1 %copy-done.13 = f32[768,6912]{1,0:T(8,128)} copy-done((f32[768,6912]{1,0:T(8,128)}, f32[768,6912]{1,0:T(8,128)S(1)}, u32[]{:S(2)}) %copy-start.13) | copy-done | bytes 21233688
  586.8 13.7 %slice_bitcast_fusion = (f32[2048,768]{0,1:T(8,128)}, f32[768,2048]{1,0:T(8,128)}, f32[768,2048]{1,0:T(8,128)}) fusion(f32[768,6912]{1,0:T(8,128)} %copy-done.13), kind=kLoop, calls=%fused_computation.17 | loop fusion | bytes 37748736 | tf_op jit(solution)/shard_map/transpose | solution.py:405
  600.5 6.6 %copy.28 = f32[2048,768]{1,0:T(8,128)} copy(f32[2048,768]{0,1:T(8,128)} %get-tuple-element.49) | data formatting | bytes 12582912
  (221 shorter events, 56.7 us)
Async XLA Ops:
  0.6 119.1 %copy-start = (bf16[2048,768]{1,0:T(8,128)(2,1)S(1)}, bf16[2048,768]{1,0:T(8,128)(2,1)}, u32[]{:S(2)}) copy-start(bf16[2048,768]{1,0:T(8,128)(2,1)} %param.23) | copy-start | bytes 9437188
  0.7 8.3 %copy-start.39 = (bf16[4,256,768]{2,1,0:T(8,128)(2,1)S(1)}, bf16[4,256,768]{2,1,0:T(8,128)(2,1)}, u32[]{:S(2)}) copy-start(bf16[4,256,768]{2,1,0:T(8,128)(2,1)} %param.24) | copy-start | bytes 4718596
  0.7 13.6 %copy-start.59 = (s32[4]{0:T(128)S(1)}, s32[4]{0:T(128)}, u32[]{:S(2)}) copy-start(s32[4]{0:T(128)} %param.26) | copy-start | bytes 52
  0.7 14.2 %copy-start.60 = (s32[4]{0:T(128)S(1)}, s32[4]{0:T(128)}, u32[]{:S(2)}) copy-start(s32[4]{0:T(128)} %param.25) | copy-start | bytes 52
  3.4 14.1 %collective-permute-start = (bf16[256,768]{1,0:T(8,128)(2,1)}, bf16[256,768]{1,0:T(8,128)(2,1)}, u32[]{:S(2)}, u32[]{:S(2)}) collective-permute-start(bf16[256,768]{1,0:T(8,128)(2,1)} %get-tuple-element.87), channel_id=1, source_target_pairs={{0,1},{1,0},{2,3},{3,2},{4,5},{5,4},{6,7},{7,6},{8,9},{9,8},{10,11... | collective-permute-start | bytes 1179656 | tf_op jit(solution)/shard_map/ppermute | solution.py:266
  6.4 21.3 %collective-permute-start.2 = (bf16[256,768]{1,0:T(8,128)(2,1)}, bf16[256,768]{1,0:T(8,128)(2,1)}, u32[]{:S(2)}, u32[]{:S(2)}) collective-permute-start(bf16[256,768]{1,0:T(8,128)(2,1)} %get-tuple-element.88), channel_id=1, source_target_pairs={{0,3},{1,2},{2,1},{3,0},{4,7},{5,6},{6,5},{7,4},{8,11},{9,10},{10,... | collective-permute-start | bytes 1179656 | tf_op jit(solution)/shard_map/ppermute | solution.py:266
  8.9 52.5 %collective-permute-start.1 = (bf16[256,768]{1,0:T(8,128)(2,1)}, bf16[256,768]{1,0:T(8,128)(2,1)}, u32[]{:S(2)}, u32[]{:S(2)}) collective-permute-start(bf16[256,768]{1,0:T(8,128)(2,1)} %get-tuple-element.89), channel_id=1, source_target_pairs={{0,2},{1,3},{2,0},{3,1},{4,6},{5,7},{6,4},{7,5},{8,10},{9,11},{10,... | collective-permute-start | bytes 1179656 | tf_op jit(solution)/shard_map/ppermute | solution.py:266
  10.0 59.6 %collective-permute-start.6 = (bf16[256,768]{1,0:T(8,128)(2,1)}, bf16[256,768]{1,0:T(8,128)(2,1)}, u32[]{:S(2)}, u32[]{:S(2)}) collective-permute-start(bf16[256,768]{1,0:T(8,128)(2,1)} %get-tuple-element.71), channel_id=1, source_target_pairs={{0,1},{1,0},{2,3},{3,2},{4,5},{5,4},{6,7},{7,6},{8,9},{9,8},{10,11... | collective-permute-start | bytes 1179656 | tf_op jit(solution)/shard_map/ppermute | solution.py:266
  11.8 57.8 %collective-permute-start.8 = (bf16[256,768]{1,0:T(8,128)(2,1)}, bf16[256,768]{1,0:T(8,128)(2,1)}, u32[]{:S(2)}, u32[]{:S(2)}) collective-permute-start(bf16[256,768]{1,0:T(8,128)(2,1)} %get-tuple-element.72), channel_id=1, source_target_pairs={{0,3},{1,2},{2,1},{3,0},{4,7},{5,6},{6,5},{7,4},{8,11},{9,10},{10,... | collective-permute-start | bytes 1179656 | tf_op jit(solution)/shard_map/ppermute | solution.py:266
  17.5 59.5 %collective-permute-start.7 = (bf16[256,768]{1,0:T(8,128)(2,1)}, bf16[256,768]{1,0:T(8,128)(2,1)S(1)}, u32[]{:S(2)}, u32[]{:S(2)}) collective-permute-start(bf16[256,768]{1,0:T(8,128)(2,1)} %get-tuple-element.73), channel_id=1, source_target_pairs={{0,2},{1,3},{2,0},{3,1},{4,6},{5,7},{6,4},{7,5},{8,10},{9,11},{10,... | collective-permute-start | bytes 1179656 | tf_op jit(solution)/shard_map/ppermute | solution.py:266
  63.1 40.5 %copy-start.21 = (bf16[256,768]{1,0:T(8,128)(2,1)}, bf16[256,768]{1,0:T(8,128)(2,1)S(1)}, u32[]{:S(2)}) copy-start(bf16[256,768]{1,0:T(8,128)(2,1)S(1)} %get-tuple-element.82) | copy-start | bytes 1179652
  63.1 40.5 %copy-start.23 = (bf16[256,768]{1,0:T(8,128)(2,1)}, bf16[256,768]{1,0:T(8,128)(2,1)S(1)}, u32[]{:S(2)}) copy-start(bf16[256,768]{1,0:T(8,128)(2,1)S(1)} %get-tuple-element.83) | copy-start | bytes 1179652
  63.1 40.5 %copy-start.27 = (bf16[256,768]{1,0:T(8,128)(2,1)}, bf16[256,768]{1,0:T(8,128)(2,1)S(1)}, u32[]{:S(2)}) copy-start(bf16[256,768]{1,0:T(8,128)(2,1)S(1)} %get-tuple-element.84) | copy-start | bytes 1179652
  63.2 40.5 %copy-start.30 = (bf16[256,768]{1,0:T(8,128)(2,1)}, bf16[256,768]{1,0:T(8,128)(2,1)S(1)}, u32[]{:S(2)}) copy-start(bf16[256,768]{1,0:T(8,128)(2,1)S(1)} %get-tuple-element.85) | copy-start | bytes 1179652
  66.3 13.3 %copy-start.1 = (bf16[1024,768]{1,0:T(8,128)(2,1)}, bf16[1024,768]{1,0:T(8,128)(2,1)S(1)}, u32[]{:S(2)}) copy-start(bf16[1024,768]{1,0:T(8,128)(2,1)S(1)} %convolution_convert_fusion.5.k_ref) | copy-start | bytes 4718596
  68.1 11.5 %copy-start.3 = (bf16[1024,768]{1,0:T(8,128)(2,1)}, bf16[1024,768]{1,0:T(8,128)(2,1)S(1)}, u32[]{:S(2)}) copy-start(bf16[1024,768]{1,0:T(8,128)(2,1)S(1)} %convolution_convert_fusion.4.v_ref) | copy-start | bytes 4718596
  69.6 10.0 %copy-start.5 = (bf16[1024,768]{1,0:T(8,128)(2,1)}, bf16[1024,768]{1,0:T(8,128)(2,1)S(1)}, u32[]{:S(2)}) copy-start(bf16[1024,768]{1,0:T(8,128)(2,1)S(1)} %convolution_convert_fusion.6.q_ref) | copy-start | bytes 4718596
  79.5 24.2 %copy-start.52 = (bf16[768,768]{1,0:T(8,128)(2,1)S(1)}, bf16[768,768]{1,0:T(8,128)(2,1)}, u32[]{:S(2)}) copy-start(bf16[768,768]{1,0:T(8,128)(2,1)} %param.19) | copy-start | bytes 3538948
  105.3 50.7 %copy-start.19 = (f32[1024,768]{1,0:T(8,128)}, f32[1024,768]{1,0:T(8,128)S(1)}, u32[]{:S(2)}) copy-start(f32[1024,768]{1,0:T(8,128)S(1)} %get-tuple-element.91) | copy-start | bytes 9437188
  135.8 6.3 %copy-start.49 = (bf16[768,2048]{1,0:T(8,128)(2,1)S(1)}, bf16[768,2048]{1,0:T(8,128)(2,1)}, u32[]{:S(2)}) copy-start(bf16[768,2048]{1,0:T(8,128)(2,1)} %param.21) | copy-start | bytes 9437188
  173.2 9.1 %collective-permute-start.22 = (bf16[384,6912]{1,0:T(8,128)(2,1)}, bf16[384,6912]{1,0:T(8,128)(2,1)}, u32[]{:S(2)}, u32[]{:S(2)}) collective-permute-start(bf16[384,6912]{1,0:T(8,128)(2,1)} %dynamic-slice_bitcast_fusion), channel_id=1, source_target_pairs={{0,4},{4,0},{8,12},{12,8},{16,20},{20,16},{24,28},{28,24},{1,5},{5... | collective-permute-start | bytes 15925256 | tf_op jit(solution)/shard_map/ppermute | solution.py:295
  191.6 59.9 %collective-permute-start.23 = (bf16[192,6912]{1,0:T(8,128)(2,1)}, bf16[192,6912]{1,0:T(8,128)(2,1)}, u32[]{:S(2)}, u32[]{:S(2)}) collective-permute-start(bf16[192,6912]{1,0:T(8,128)(2,1)} %dynamic-slice_bitcast_fusion.1), channel_id=1, source_target_pairs={{0,8},{4,12},{8,0},{12,4},{16,24},{20,28},{24,16},{28,20},{1,9},{5... | collective-permute-start | bytes 7962632 | tf_op jit(solution)/shard_map/ppermute | solution.py:295
  196.9 54.6 %copy-start.16 = (bf16[384,6912]{1,0:T(8,128)(2,1)S(1)}, bf16[384,6912]{1,0:T(8,128)(2,1)}, u32[]{:S(2)}) copy-start(bf16[384,6912]{1,0:T(8,128)(2,1)} %copy-done.15) | copy-start | bytes 15925252
  230.9 24.7 %copy-start.9 = (bf16[1024,768]{1,0:T(8,128)(2,1)}, bf16[1024,768]{1,0:T(8,128)(2,1)S(1)}, u32[]{:S(2)}) copy-start(bf16[1024,768]{1,0:T(8,128)(2,1)S(1)} %get-tuple-element.18) | copy-start | bytes 4718596
  230.9 26.3 %copy-start.11 = (bf16[1024,768]{1,0:T(8,128)(2,1)}, bf16[1024,768]{1,0:T(8,128)(2,1)S(1)}, u32[]{:S(2)}) copy-start(bf16[1024,768]{1,0:T(8,128)(2,1)S(1)} %get-tuple-element.19) | copy-start | bytes 4718596
  230.9 27.9 %copy-start.7 = (bf16[1024,768]{1,0:T(8,128)(2,1)}, bf16[1024,768]{1,0:T(8,128)(2,1)S(1)}, u32[]{:S(2)}) copy-start(bf16[1024,768]{1,0:T(8,128)(2,1)S(1)} %get-tuple-element.20) | copy-start | bytes 4718596
  230.9 24.6 %copy-start.22 = (bf16[256,768]{1,0:T(8,128)(2,1)S(1)}, bf16[256,768]{1,0:T(8,128)(2,1)}, u32[]{:S(2)}) copy-start(bf16[256,768]{1,0:T(8,128)(2,1)} %copy-done.21) | copy-start | bytes 1179652
  230.9 24.6 %copy-start.24 = (bf16[256,768]{1,0:T(8,128)(2,1)S(1)}, bf16[256,768]{1,0:T(8,128)(2,1)}, u32[]{:S(2)}) copy-start(bf16[256,768]{1,0:T(8,128)(2,1)} %copy-done.23) | copy-start | bytes 1179652
  230.9 24.6 %copy-start.28 = (bf16[256,768]{1,0:T(8,128)(2,1)S(1)}, bf16[256,768]{1,0:T(8,128)(2,1)}, u32[]{:S(2)}) copy-start(bf16[256,768]{1,0:T(8,128)(2,1)} %copy-done.27) | copy-start | bytes 1179652
  231.0 24.6 %copy-start.31 = (bf16[256,768]{1,0:T(8,128)(2,1)S(1)}, bf16[256,768]{1,0:T(8,128)(2,1)}, u32[]{:S(2)}) copy-start(bf16[256,768]{1,0:T(8,128)(2,1)} %copy-done.30) | copy-start | bytes 1179652
  254.0 30.4 %collective-permute-start.24 = (bf16[96,6912]{1,0:T(8,128)(2,1)S(1)}, bf16[96,6912]{1,0:T(8,128)(2,1)S(1)}, u32[]{:S(2)}, u32[]{:S(2)}) collective-permute-start(bf16[96,6912]{1,0:T(8,128)(2,1)S(1)} %dynamic-slice_bitcast_fusion.3), channel_id=1, source_target_pairs={{0,16},{4,20},{8,24},{12,28},{16,0},{20,4},{24,8},{28,12},{1,17},{... | collective-permute-start | bytes 3981320 | tf_op jit(solution)/shard_map/ppermute | solution.py:295
  284.7 15.3 %collective-permute-start.25 = (bf16[48,6912]{1,0:T(8,128)(2,1)S(1)}, bf16[48,6912]{1,0:T(8,128)(2,1)S(1)}, u32[]{:S(2)}, u32[]{:S(2)}) collective-permute-start(bf16[48,6912]{1,0:T(8,128)(2,1)S(1)} %dynamic-slice_bitcast_fusion.5), channel_id=1, source_target_pairs={{0,1},{1,0},{2,3},{3,2},{4,5},{5,4},{6,7},{7,6},{8,9},{9,8},{10,11... | collective-permute-start | bytes 1990664 | tf_op jit(solution)/shard_map/ppermute | solution.py:295
  285.2 16.5 %collective-permute-start.12 = (bf16[384,2304]{1,0:T(8,128)(2,1)S(1)}, bf16[384,2304]{1,0:T(8,128)(2,1)S(1)}, u32[]{:S(2)}, u32[]{:S(2)}) collective-permute-start(bf16[384,2304]{1,0:T(8,128)(2,1)S(1)} %dynamic-slice_bitcast_fusion.2), channel_id=1, source_target_pairs={{0,4},{4,0},{8,12},{12,8},{16,20},{20,16},{24,28},{28,24},{1,5},{5... | collective-permute-start | bytes 5308424 | tf_op jit(solution)/shard_map/ppermute | solution.py:295
  300.2 15.2 %collective-permute-start.26 = (bf16[24,6912]{1,0:T(8,128)(2,1)S(1)}, bf16[24,6912]{1,0:T(8,128)(2,1)S(1)}, u32[]{:S(2)}, u32[]{:S(2)}) collective-permute-start(bf16[24,6912]{1,0:T(8,128)(2,1)S(1)} %dynamic-slice_bitcast_fusion.27), channel_id=1, source_target_pairs={{0,2},{1,3},{2,0},{3,1},{4,6},{5,7},{6,4},{7,5},{8,10},{9,11},{10,... | collective-permute-start | bytes 995336 | tf_op jit(solution)/shard_map/ppermute | solution.py:295
  302.3 14.0 %copy-start.20 = (bf16[384,2304]{1,0:T(8,128)(2,1)}, bf16[384,2304]{1,0:T(8,128)(2,1)S(1)}, u32[]{:S(2)}) copy-start(bf16[384,2304]{1,0:T(8,128)(2,1)S(1)} %fusion.13) | copy-start | bytes 5308420
  316.3 18.0 %collective-permute-start.27 = (bf16[24,6912]{1,0:T(8,128)(2,1)}, bf16[24,6912]{1,0:T(8,128)(2,1)}, u32[]{:S(2)}, u32[]{:S(2)}) collective-permute-start(bf16[24,6912]{1,0:T(8,128)(2,1)} %fusion.27), channel_id=1, source_target_pairs={{0,2},{1,3},{2,0},{3,1},{4,6},{5,7},{6,4},{7,5},{8,10},{9,11},{10,... | collective-permute-start | bytes 995336 | tf_op jit(solution)/shard_map/ppermute | solution.py:303
  317.3 21.9 %collective-permute-start.13 = (bf16[192,2304]{1,0:T(8,128)(2,1)}, bf16[192,2304]{1,0:T(8,128)(2,1)}, u32[]{:S(2)}, u32[]{:S(2)}) collective-permute-start(bf16[192,2304]{1,0:T(8,128)(2,1)} %dynamic-slice_bitcast_fusion.4), channel_id=1, source_target_pairs={{0,16},{4,20},{8,24},{12,28},{16,0},{20,4},{24,8},{28,12},{1,17},{... | collective-permute-start | bytes 2654216 | tf_op jit(solution)/shard_map/ppermute | solution.py:295
  335.7 16.9 %collective-permute-start.28 = (bf16[48,6912]{1,0:T(8,128)(2,1)S(1)}, bf16[48,6912]{1,0:T(8,128)(2,1)S(1)}, u32[]{:S(2)}, u32[]{:S(2)}) collective-permute-start(bf16[48,6912]{1,0:T(8,128)(2,1)S(1)} %maximum_select_fusion.7), channel_id=1, source_target_pairs={{0,1},{1,0},{2,3},{3,2},{4,5},{5,4},{6,7},{7,6},{8,9},{9,8},{10,11... | collective-permute-start | bytes 1990664 | tf_op jit(solution)/shard_map/ppermute | solution.py:303
  340.8 14.6 %collective-permute-start.14 = (bf16[96,2304]{1,0:T(8,128)(2,1)S(1)}, bf16[96,2304]{1,0:T(8,128)(2,1)S(1)}, u32[]{:S(2)}, u32[]{:S(2)}) collective-permute-start(bf16[96,2304]{1,0:T(8,128)(2,1)S(1)} %dynamic-slice_bitcast_fusion.6), channel_id=1, source_target_pairs={{0,8},{4,12},{8,0},{12,4},{16,24},{20,28},{24,16},{28,20},{1,9},{5... | collective-permute-start | bytes 1327112 | tf_op jit(solution)/shard_map/ppermute | solution.py:295
  353.9 30.5 %collective-permute-start.29 = (bf16[96,6912]{1,0:T(8,128)(2,1)}, bf16[96,6912]{1,0:T(8,128)(2,1)}, u32[]{:S(2)}, u32[]{:S(2)}) collective-permute-start(bf16[96,6912]{1,0:T(8,128)(2,1)} %maximum_select_fusion.5), channel_id=1, source_target_pairs={{0,16},{4,20},{8,24},{12,28},{16,0},{20,4},{24,8},{28,12},{1,17},{... | collective-permute-start | bytes 3981320 | tf_op jit(solution)/shard_map/ppermute | solution.py:303
  357.0 6.5 %collective-permute-start.15 = (bf16[48,2304]{1,0:T(8,128)(2,1)}, bf16[48,2304]{1,0:T(8,128)(2,1)}, u32[]{:S(2)}, u32[]{:S(2)}) collective-permute-start(bf16[48,2304]{1,0:T(8,128)(2,1)} %dynamic-slice_bitcast_fusion.28), channel_id=1, source_target_pairs={{0,1},{1,0},{2,3},{3,2},{4,5},{5,4},{6,7},{7,6},{8,9},{9,8},{10,11... | collective-permute-start | bytes 663560 | tf_op jit(solution)/shard_map/ppermute | solution.py:295
  388.7 60.9 %collective-permute-start.30 = (bf16[192,6912]{1,0:T(8,128)(2,1)}, bf16[192,6912]{1,0:T(8,128)(2,1)}, u32[]{:S(2)}, u32[]{:S(2)}) collective-permute-start(bf16[192,6912]{1,0:T(8,128)(2,1)} %maximum_select_fusion.3), channel_id=1, source_target_pairs={{0,8},{4,12},{8,0},{12,4},{16,24},{20,28},{24,16},{28,20},{1,9},{5... | collective-permute-start | bytes 7962632 | tf_op jit(solution)/shard_map/ppermute | solution.py:303
  390.3 6.9 %collective-permute-start.16 = (bf16[24,2304]{1,0:T(8,128)(2,1)S(1)}, bf16[24,2304]{1,0:T(8,128)(2,1)S(1)}, u32[]{:S(2)}, u32[]{:S(2)}) collective-permute-start(bf16[24,2304]{1,0:T(8,128)(2,1)S(1)} %dynamic-slice_bitcast_fusion.29), channel_id=1, source_target_pairs={{0,2},{1,3},{2,0},{3,1},{4,6},{5,7},{6,4},{7,5},{8,10},{9,11},{10,... | collective-permute-start | bytes 331784 | tf_op jit(solution)/shard_map/ppermute | solution.py:295
  397.8 6.1 %collective-permute-start.17 = (bf16[24,2304]{1,0:T(8,128)(2,1)}, bf16[24,2304]{1,0:T(8,128)(2,1)}, u32[]{:S(2)}, u32[]{:S(2)}) collective-permute-start(bf16[24,2304]{1,0:T(8,128)(2,1)} %fusion.29), channel_id=1, source_target_pairs={{0,2},{1,3},{2,0},{3,1},{4,6},{5,7},{6,4},{7,5},{8,10},{9,11},{10,... | collective-permute-start | bytes 331784 | tf_op jit(solution)/shard_map/ppermute | solution.py:303
  405.1 6.7 %collective-permute-start.18 = (bf16[48,2304]{1,0:T(8,128)(2,1)S(1)}, bf16[48,2304]{1,0:T(8,128)(2,1)S(1)}, u32[]{:S(2)}, u32[]{:S(2)}) collective-permute-start(bf16[48,2304]{1,0:T(8,128)(2,1)S(1)} %maximum_select_fusion.9), channel_id=1, source_target_pairs={{0,1},{1,0},{2,3},{3,2},{4,5},{5,4},{6,7},{7,6},{8,9},{9,8},{10,11... | collective-permute-start | bytes 663560 | tf_op jit(solution)/shard_map/ppermute | solution.py:303
  411.8 45.4 %copy-start.12 = (bf16[1024,768]{1,0:T(8,128)(2,1)S(1)}, bf16[1024,768]{1,0:T(8,128)(2,1)}, u32[]{:S(2)}) copy-start(bf16[1024,768]{1,0:T(8,128)(2,1)} %copy-done.11) | copy-start | bytes 4718596
  411.8 45.4 %copy-start.54 = (bf16[768,768]{1,0:T(8,128)(2,1)S(1)}, bf16[768,768]{1,0:T(8,128)(2,1)}, u32[]{:S(2)}) copy-start(bf16[768,768]{1,0:T(8,128)(2,1)} %param.17) | copy-start | bytes 3538948
  411.8 48.5 %collective-permute-start.19 = (bf16[96,2304]{1,0:T(8,128)(2,1)S(1)}, bf16[96,2304]{1,0:T(8,128)(2,1)S(1)}, u32[]{:S(2)}, u32[]{:S(2)}) collective-permute-start(bf16[96,2304]{1,0:T(8,128)(2,1)S(1)} %maximum_select_fusion.8), channel_id=1, source_target_pairs={{0,8},{4,12},{8,0},{12,4},{16,24},{20,28},{24,16},{28,20},{1,9},{5... | collective-permute-start | bytes 1327112 | tf_op jit(solution)/shard_map/ppermute | solution.py:303
  457.1 112.0 %collective-permute-start.31 = (bf16[384,6912]{1,0:T(8,128)(2,1)}, bf16[384,6912]{1,0:T(8,128)(2,1)}, u32[]{:S(2)}, u32[]{:S(2)}) collective-permute-start(bf16[384,6912]{1,0:T(8,128)(2,1)} %maximum_select_fusion.1), channel_id=1, source_target_pairs={{0,4},{4,0},{8,12},{12,8},{16,20},{20,16},{24,28},{28,24},{1,5},{5... | collective-permute-start | bytes 15925256 | tf_op jit(solution)/shard_map/ppermute | solution.py:303
  460.3 8.2 %copy-start.8 = (bf16[1024,768]{1,0:T(8,128)(2,1)S(1)}, bf16[1024,768]{1,0:T(8,128)(2,1)}, u32[]{:S(2)}) copy-start(bf16[1024,768]{1,0:T(8,128)(2,1)} %copy-done.7) | copy-start | bytes 4718596
  460.3 8.2 %copy-start.25 = (bf16[256,768]{1,0:T(8,128)(2,1)S(1)}, bf16[256,768]{1,0:T(8,128)(2,1)}, u32[]{:S(2)}) copy-start(bf16[256,768]{1,0:T(8,128)(2,1)} %copy-done.23) | copy-start | bytes 1179652
  460.3 8.2 %copy-start.29 = (bf16[256,768]{1,0:T(8,128)(2,1)S(1)}, bf16[256,768]{1,0:T(8,128)(2,1)}, u32[]{:S(2)}) copy-start(bf16[256,768]{1,0:T(8,128)(2,1)} %copy-done.27) | copy-start | bytes 1179652
  460.3 8.2 %copy-start.32 = (bf16[256,768]{1,0:T(8,128)(2,1)S(1)}, bf16[256,768]{1,0:T(8,128)(2,1)}, u32[]{:S(2)}) copy-start(bf16[256,768]{1,0:T(8,128)(2,1)} %copy-done.30) | copy-start | bytes 1179652
  460.3 8.2 %copy-start.58 = (bf16[768,768]{1,0:T(8,128)(2,1)S(1)}, bf16[768,768]{1,0:T(8,128)(2,1)}, u32[]{:S(2)}) copy-start(bf16[768,768]{1,0:T(8,128)(2,1)} %param.18) | copy-start | bytes 3538948
  461.4 58.6 %collective-permute-start.20 = (bf16[192,2304]{1,0:T(8,128)(2,1)}, bf16[192,2304]{1,0:T(8,128)(2,1)}, u32[]{:S(2)}, u32[]{:S(2)}) collective-permute-start(bf16[192,2304]{1,0:T(8,128)(2,1)} %maximum_select_fusion.6), channel_id=1, source_target_pairs={{0,16},{4,20},{8,24},{12,28},{16,0},{20,4},{24,8},{28,12},{1,17},{... | collective-permute-start | bytes 2654216 | tf_op jit(solution)/shard_map/ppermute | solution.py:303
  464.1 62.8 %collective-permute-start.5 = (bf16[256,768]{1,0:T(8,128)(2,1)}, bf16[256,768]{1,0:T(8,128)(2,1)}, u32[]{:S(2)}, u32[]{:S(2)}) collective-permute-start(bf16[256,768]{1,0:T(8,128)(2,1)} %get-tuple-element.79), channel_id=1, source_target_pairs={{0,3},{1,2},{2,1},{3,0},{4,7},{5,6},{6,5},{7,4},{8,11},{9,10},{10,... | collective-permute-start | bytes 1179656 | tf_op jit(solution)/shard_map/ppermute | solution.py:277
  465.3 63.9 %collective-permute-start.4 = (bf16[256,768]{1,0:T(8,128)(2,1)}, bf16[256,768]{1,0:T(8,128)(2,1)}, u32[]{:S(2)}, u32[]{:S(2)}) collective-permute-start(bf16[256,768]{1,0:T(8,128)(2,1)} %get-tuple-element.80), channel_id=1, source_target_pairs={{0,2},{1,3},{2,0},{3,1},{4,6},{5,7},{6,4},{7,5},{8,10},{9,11},{10,... | collective-permute-start | bytes 1179656 | tf_op jit(solution)/shard_map/ppermute | solution.py:277
  466.2 63.1 %collective-permute-start.3 = (bf16[256,768]{1,0:T(8,128)(2,1)}, bf16[256,768]{1,0:T(8,128)(2,1)}, u32[]{:S(2)}, u32[]{:S(2)}) collective-permute-start(bf16[256,768]{1,0:T(8,128)(2,1)} %get-tuple-element.81), channel_id=1, source_target_pairs={{0,1},{1,0},{2,3},{3,2},{4,5},{5,4},{6,7},{7,6},{8,9},{9,8},{10,11... | collective-permute-start | bytes 1179656 | tf_op jit(solution)/shard_map/ppermute | solution.py:277
  474.5 48.1 %copy-start.44 = (f32[1024]{0:T(1024)S(1)}, f32[1024]{0:T(1024)}, u32[]{:S(2)}) copy-start(f32[1024]{0:T(1024)} %copy-done.43) | copy-start | bytes 12292
  522.5 42.7 %collective-permute-start.21 = (bf16[384,2304]{1,0:T(8,128)(2,1)S(1)}, bf16[384,2304]{1,0:T(8,128)(2,1)S(1)}, u32[]{:S(2)}, u32[]{:S(2)}) collective-permute-start(bf16[384,2304]{1,0:T(8,128)(2,1)S(1)} %maximum_select_fusion.4), channel_id=1, source_target_pairs={{0,4},{4,0},{8,12},{12,8},{16,20},{20,16},{24,28},{28,24},{1,5},{5... | collective-permute-start | bytes 5308424 | tf_op jit(solution)/shard_map/ppermute | solution.py:303
  526.8 13.9 %collective-permute-start.11 = (bf16[256,768]{1,0:T(8,128)(2,1)S(1)}, bf16[256,768]{1,0:T(8,128)(2,1)S(1)}, u32[]{:S(2)}, u32[]{:S(2)}) collective-permute-start(bf16[256,768]{1,0:T(8,128)(2,1)S(1)} %get-tuple-element.63), channel_id=1, source_target_pairs={{0,3},{1,2},{2,1},{3,0},{4,7},{5,6},{6,5},{7,4},{8,11},{9,10},{10,... | collective-permute-start | bytes 1179656 | tf_op jit(solution)/shard_map/ppermute | solution.py:277
  529.2 33.8 %collective-permute-start.10 = (bf16[256,768]{1,0:T(8,128)(2,1)S(1)}, bf16[256,768]{1,0:T(8,128)(2,1)S(1)}, u32[]{:S(2)}, u32[]{:S(2)}) collective-permute-start(bf16[256,768]{1,0:T(8,128)(2,1)S(1)} %get-tuple-element.64), channel_id=1, source_target_pairs={{0,2},{1,3},{2,0},{3,1},{4,6},{5,7},{6,4},{7,5},{8,10},{9,11},{10,... | collective-permute-start | bytes 1179656 | tf_op jit(solution)/shard_map/ppermute | solution.py:277
  529.2 33.8 %collective-permute-start.9 = (bf16[256,768]{1,0:T(8,128)(2,1)S(1)}, bf16[256,768]{1,0:T(8,128)(2,1)S(1)}, u32[]{:S(2)}, u32[]{:S(2)}) collective-permute-start(bf16[256,768]{1,0:T(8,128)(2,1)S(1)} %get-tuple-element.65), channel_id=1, source_target_pairs={{0,1},{1,0},{2,3},{3,2},{4,5},{5,4},{6,7},{7,6},{8,9},{9,8},{10,11... | collective-permute-start | bytes 1179656 | tf_op jit(solution)/shard_map/ppermute | solution.py:277
  578.1 7.1 %copy-start.13 = (f32[768,6912]{1,0:T(8,128)}, f32[768,6912]{1,0:T(8,128)S(1)}, u32[]{:S(2)}) copy-start(f32[768,6912]{1,0:T(8,128)S(1)} %fusion) | copy-start | bytes 63700996
  (33 other events, 117.4 us)
